TPU v7x, 256 devices: a whole 4x4x8 slice. The times are simulated.
256 devices in a mesh: prow: 32 (over z, x), pcol: 8 (over y, core).
Axes of the slice: x: 4, y: 4, z: 8, core: 2. Of those that a mesh axis runs over, the one named last changes fastest.
Arguments:
- root_cov: float32 [4096, 4096], P('prow', 'pcol'), as said below
- row_blocks: int32 [4, 16], replicated, may hold values from 8 to 63, as said below
- lhat_t: float32 [4, 1024, 2048], P(None, 'prow', 'pcol'), may hold values from -0.25 to 0.25
- diag_inv: float32 [4, 1024, 1024], P(None, None, 'pcol'), as said below
Outputs:
- row_panels: float32 [4, 1024, 2048], P(None, None, 'pcol')
- diag_blocks: float32 [4, 1024, 1024], P(None, None, 'pcol')
Inputs may be any that keep to these rules, and one draw needn't show every extreme that they name: `row_blocks`: each row lists 16 distinct blocks. Row 0 holds blocks of the ancestor region only, two of each residue modulo 8, always including block 63; row k > 0 holds all 8 blocks of supernode k - 1 and one block of each residue modulo 8 from row k - 1. Within a row the blocks are ordered by residue modulo 8, then ascending. `root_cov`: symmetric with a positive diagonal. `diag_inv`: each supernode's block is symmetric with a positive diagonal.
All inputs are finite; a program needn't handle non-finite values.
Results may differ from a plain program's by a relative error of at most 0.00012.
Values sent between devices are 32-bit elements; how exact they have to be, the bound alone decides.
A program may use at most 64 MiB of HBM per device.

v0:
```python
import jax
import jax.numpy as jnp
from jax import lax
from jax.sharding import PartitionSpec as P

BLOCK = 128
SUPER_BLOCKS = 8
SUPERS = 4
NB = 64
W = 1024
K = 16


def spread(block, axis, holder):
    block = jnp.where(lax.axis_index(axis) == holder, block, jnp.zeros_like(block))
    return lax.psum(block, axis)


def on_device(root_cov, row_blocks, lhat_t, diag_inv):
    high = lax.Precision.HIGHEST
    nrow = lax.axis_size("prow")
    ncol = lax.axis_size("pcol")
    prow_id = lax.axis_index("prow")
    pcol_id = lax.axis_index("pcol")
    loc_rows = NB // nrow
    loc_cols = NB // ncol
    per_col = K // ncol
    sup_col = SUPER_BLOCKS // ncol
    sigma = jnp.zeros((loc_rows * BLOCK, loc_cols * BLOCK), jnp.float32)
    sigma = lax.dynamic_update_slice(
        sigma,
        root_cov,
        (SUPERS * SUPER_BLOCKS // nrow * BLOCK, SUPERS * SUPER_BLOCKS // ncol * BLOCK),
    )
    block_rows = jnp.arange(loc_rows, dtype=jnp.int32) * nrow + prow_id
    owner = prow_id % ncol
    slots = jnp.arange(SUPER_BLOCKS, dtype=jnp.int32)
    natural_ordering = slots % sup_col * ncol + slots // sup_col
    panels = []
    diagonal_list = []
    for k in range(SUPERS):
        start = (SUPERS - 1 - k) * SUPER_BLOCKS
        blocks = row_blocks[k]
        mine = lax.dynamic_slice_in_dim(blocks, pcol_id * per_col, per_col)
        theirs = lax.dynamic_slice_in_dim(blocks, owner * per_col, per_col)
        col_local = mine // ncol
        lhat_class = lax.all_gather(lhat_t[k], "prow", axis=0, tiled=True)
        lhat_owner = spread(lhat_class, "pcol", owner)
        chosen = (block_rows[:, None] == theirs[None, :]).astype(jnp.float32)
        lsel_t = jnp.einsum(
            "wjr,lj->wlr", lhat_owner.reshape(W, per_col, BLOCK), chosen, precision=high
        ).reshape(W, loc_rows * BLOCK)
        columns = jnp.take(sigma.reshape(loc_rows * BLOCK, loc_cols, BLOCK), col_local, axis=1)
        columns = columns.reshape(loc_rows * BLOCK, per_col * BLOCK)
        row_part = jnp.dot(lsel_t, columns, precision=high)
        col_part = lax.dot_general(columns, lhat_class, (((1,), (1,)), ((), ())), precision=high)
        summed = lax.psum_scatter(col_part, "pcol", scatter_dimension=1, tiled=True)
        in_rows = jnp.any(block_rows[:, None] == blocks[None, :], axis=1).astype(jnp.float32)
        panel_loc = -summed * jnp.repeat(in_rows, BLOCK)[:, None]
        diag_part = jnp.dot(lsel_t, panel_loc, precision=high)
        row_sum, diag_sum = lax.psum((row_part, diag_part), "prow")
        turned = -row_sum
        diag_new = diag_inv[k] - diag_sum
        panels.append(turned)
        diagonal_list.append(diag_new)
        first_col = start // ncol
        sigma = lax.dynamic_update_slice(sigma, panel_loc, (0, first_col * BLOCK))
        hit = (block_rows[:, None] == start + natural_ordering[None, :]).astype(jnp.float32)
        has_row = jnp.sum(hit, axis=1) > 0.5
        row_source = jnp.concatenate([turned, diag_new], axis=1)
        new_rows = jnp.einsum(
            "lt,trc->lrc",
            hit,
            row_source.reshape(SUPER_BLOCKS, BLOCK, (per_col + sup_col) * BLOCK),
            precision=high,
        )
        grid = sigma.reshape(loc_rows, BLOCK, loc_cols, BLOCK)
        new_front = new_rows[:, :, : per_col * BLOCK].reshape(loc_rows, BLOCK, per_col, BLOCK)
        old_front = jnp.take(grid, col_local, axis=2)
        grid = grid.at[:, :, col_local].set(
            jnp.where(has_row[:, None, None, None], new_front, old_front)
        )
        new_diag = new_rows[:, :, per_col * BLOCK :].reshape(loc_rows, BLOCK, sup_col, BLOCK)
        old_diag = grid[:, :, first_col : first_col + sup_col]
        grid = grid.at[:, :, first_col : first_col + sup_col].set(
            jnp.where(has_row[:, None, None, None], new_diag, old_diag)
        )
        sigma = grid.reshape(loc_rows * BLOCK, loc_cols * BLOCK)
    return (jnp.stack(panels), jnp.stack(diagonal_list))


def solution(mesh):
    return jax.shard_map(
        on_device,
        mesh=mesh,
        in_specs=(P("prow", "pcol"), P(), P(None, "prow", "pcol"), P(None, None, "pcol")),
        out_specs=(P(None, None, "pcol"), P(None, None, "pcol")),
        check_vma=False,
    )
```

profile of v0, /device:TPU:1, one launch (start us, length us, event | category | flops | bytes accessed | tf_op | source)
XLA Modules:
  0.0 1205.7 jit_solution(12487918274711008056)
XLA Ops:
  10.8 75.9 %all-gather.9.cloned.1.call-done = f32[1,1024,256]{2,1,0:T(8,128)} async-done(((f32[1,32,256]{2,1,0:T(8,128)}), f32[1,1024,256]{2,1,0:T(8,128)}) %all-gather.9.cloned.1.call-update) | async-done | bytes 1048592 | tf_op jit(solution)/shard_map/all_gather | solution.py:47
  89.5 73.6 %all-gather.11.cloned.1.call-done = f32[1,1024,256]{2,1,0:T(8,128)} async-done(((f32[1,32,256]{2,1,0:T(8,128)}), f32[1,1024,256]{2,1,0:T(8,128)}) %all-gather.11.cloned.1.call-update) | async-done | bytes 1048592 | tf_op jit(solution)/shard_map/all_gather | solution.py:47
  166.1 73.5 %all-gather.13.cloned.1.call-done = f32[1,1024,256]{2,1,0:T(8,128)} async-done(((f32[1,32,256]{2,1,0:T(8,128)}), f32[1,1024,256]{2,1,0:T(8,128)}) %all-gather.13.cloned.1.call-update) | async-done | bytes 1048592 | tf_op jit(solution)/shard_map/all_gather | solution.py:47
  242.4 74.0 %all-gather.15.cloned.1.call-done = f32[1,1024,256]{2,1,0:T(8,128)} async-done(((f32[1,32,256]{2,1,0:T(8,128)}), f32[1,1024,256]{2,1,0:T(8,128)}) %all-gather.15.cloned.1.call-update) | async-done | bytes 1048592 | tf_op jit(solution)/shard_map/all_gather | solution.py:47
  323.9 2.8 fusion.28
  327.7 70.0 %all-reduce.20.cloned.1.call-done = (f32[1024,2,128]{2,1,0:T(2,128)}, f32[1024,2,128]{2,1,0:T(2,128)}, f32[1024,2,128]{2,1,0:T(2,128)}, f32[1024,2,128]{2,1,0:T(2,128)}) async-done(((f32[1024,2,128]{2,1,0:T(2,128)}, f32[1024,2,128]{2,1,0:T(2,128)}, f32[1024,2,128]{2,1,0:T(2,128)}, f32[1024,2,128]{2,1,0:T(2,128)}), (f32[1024,2,128]{2,1,0:T(2,128)}, f32[1024,2,128]{2,1,0:T(2,128)}, f32[1024,2,128]{2,1,0:T(2,128)}, ...) | async-done | bytes 4194320 | tf_op jit(solution)/shard_map/psum | solution.py:16
  397.7 3.3 fusion.58
  401.0 2.0 fusion.20
  403.0 31.5 %reduce-scatter.5.cloned.1.call-done = f32[256,128]{1,0:T(8,128)} async-done(((f32[256,1024]{1,0:T(8,128)}), f32[256,128]{1,0:T(8,128)}) %reduce-scatter.5.cloned.1.call-update) | async-done | bytes 131088 | tf_op jit(solution)/shard_map/reduce_scatter | solution.py:57
  441.9 145.5 %all-reduce.18.cloned.1.call-done = (f32[1024,128]{1,0:T(8,128)}, f32[1024,256]{1,0:T(8,128)}) async-done(((f32[1024,128]{1,0:T(8,128)}, f32[1024,256]{1,0:T(8,128)}), (f32[1024,128]{1,0:T(8,128)}, f32[1024,256]{1,0:T(8,128)})) %all-reduce.18.cloned.1.call-update) | async-done | bytes 1572880 | tf_op jit(solution)/shard_map/psum | solution.py:61
  587.4 2.4 negate_bitcast_fusion.3
  597.8 2.8 fusion.26
  600.8 3.3 fusion.56
  604.2 2.0 fusion.16
  606.2 28.1 %reduce-scatter.7.cloned.1.call-done = f32[256,128]{1,0:T(8,128)} async-done(((f32[256,1024]{1,0:T(8,128)}), f32[256,128]{1,0:T(8,128)}) %reduce-scatter.7.cloned.1.call-update) | async-done | bytes 131088 | tf_op jit(solution)/shard_map/reduce_scatter | solution.py:57
  634.3 2.8 fusion.14
  639.3 148.2 %all-reduce.16.cloned.1.call-done = (f32[1024,128]{1,0:T(8,128)}, f32[1024,256]{1,0:T(8,128)}) async-done(((f32[1024,128]{1,0:T(8,128)}, f32[1024,256]{1,0:T(8,128)}), (f32[1024,128]{1,0:T(8,128)}, f32[1024,256]{1,0:T(8,128)})) %all-reduce.16.cloned.1.call-update) | async-done | bytes 1572880 | tf_op jit(solution)/shard_map/psum | solution.py:61
  787.5 2.4 negate_bitcast_fusion.2
  799.6 2.8 fusion.24
  803.2 3.3 fusion.54
  806.6 2.0 fusion.12
  808.6 27.5 %reduce-scatter.9.cloned.1.call-done = f32[256,128]{1,0:T(8,128)} async-done(((f32[256,1024]{1,0:T(8,128)}), f32[256,128]{1,0:T(8,128)}) %reduce-scatter.9.cloned.1.call-update) | async-done | bytes 131088 | tf_op jit(solution)/shard_map/reduce_scatter | solution.py:57
  836.0 2.8 fusion.10
  841.0 147.9 %all-reduce.14.cloned.1.call-done = (f32[1024,128]{1,0:T(8,128)}, f32[1024,256]{1,0:T(8,128)}) async-done(((f32[1024,128]{1,0:T(8,128)}, f32[1024,256]{1,0:T(8,128)}), (f32[1024,128]{1,0:T(8,128)}, f32[1024,256]{1,0:T(8,128)})) %all-reduce.14.cloned.1.call-update) | async-done | bytes 1572880 | tf_op jit(solution)/shard_map/psum | solution.py:61
  988.9 2.4 negate_bitcast_fusion.1
  1002.8 2.9 fusion.22
  1005.8 3.3 fusion.52
  1009.1 2.0 fusion.8
  1011.1 28.1 %reduce-scatter.11.cloned.1.call-done = f32[256,128]{1,0:T(8,128)} async-done(((f32[256,1024]{1,0:T(8,128)}), f32[256,128]{1,0:T(8,128)}) %reduce-scatter.11.cloned.1.call-update) | async-done | bytes 131088 | tf_op jit(solution)/shard_map/reduce_scatter | solution.py:57
  1039.2 2.8 fusion.6
  1042.0 150.4 %all-reduce.12.cloned.1.call-done = (f32[1024,256]{1,0:T(8,128)}, f32[1024,128]{1,0:T(8,128)}) async-done(((f32[1024,256]{1,0:T(8,128)}, f32[1024,128]{1,0:T(8,128)}), (f32[1024,256]{1,0:T(8,128)}, f32[1024,128]{1,0:T(8,128)})) %all-reduce.12.cloned.1.call-update) | async-done | bytes 1572880 | tf_op jit(solution)/shard_map/psum | solution.py:61
  1196.6 2.3 pad_maximum_fusion
  (169 shorter events, 66.1 us)
Async XLA Ops:
  7.2 79.6 %all-gather.9.cloned.1.call-start = ((), (), s32[]{:S(2)}) async-start(), calls=%async_computation.8 | async-start | bytes 1081344 | tf_op jit(solution)/shard_map/all_gather | solution.py:47
  8.7 154.5 %all-gather.11.cloned.1.call-start = ((), (), s32[]{:S(2)}) async-start(), calls=%async_computation.9 | async-start | bytes 1081344 | tf_op jit(solution)/shard_map/all_gather | solution.py:47
  9.4 230.1 %all-gather.13.cloned.1.call-start = ((), (), s32[]{:S(2)}) async-start(), calls=%async_computation.10 | async-start | bytes 1081344 | tf_op jit(solution)/shard_map/all_gather | solution.py:47
  10.2 306.3 %all-gather.15.cloned.1.call-start = ((), (), s32[]{:S(2)}) async-start(), calls=%async_computation.11 | async-start | bytes 1081344 | tf_op jit(solution)/shard_map/all_gather | solution.py:47
  10.8 386.9 %all-reduce.20.cloned.1.call-start = ((), (), s32[]{:S(2)}) async-start(), calls=%async_computation.16 | async-start | bytes 8388608 | tf_op jit(solution)/shard_map/psum | solution.py:16
  319.2 0.9 copy-start.13
  319.3 115.2 %reduce-scatter.5.cloned.1.call-start = ((), (), s32[]{:S(2)}) async-start(), calls=%async_computation.4 | async-start | bytes 1179648 | tf_op jit(solution)/shard_map/reduce_scatter | solution.py:57
  320.3 1.4 copy-start.15
  320.4 3.5 copy-start.3
  326.7 260.6 %all-reduce.18.cloned.1.call-start = ((), (), s32[]{:S(2)}) async-start(), calls=%async_computation.15 | async-start | bytes 3145728 | tf_op jit(solution)/shard_map/psum | solution.py:61
  437.4 196.9 %reduce-scatter.7.cloned.1.call-start = ((), (), s32[]{:S(2)}) async-start(), calls=%async_computation.5 | async-start | bytes 1179648 | tf_op jit(solution)/shard_map/reduce_scatter | solution.py:57
  587.4 2.4 copy-start.8
  594.6 3.2 copy-start.2
  600.7 186.8 %all-reduce.16.cloned.1.call-start = ((), (), s32[]{:S(2)}) async-start(), calls=%async_computation.14 | async-start | bytes 3145728 | tf_op jit(solution)/shard_map/psum | solution.py:61
  637.1 1.1 copy-start.11
  637.1 199.0 %reduce-scatter.9.cloned.1.call-start = ((), (), s32[]{:S(2)}) async-start(), calls=%async_computation.6 | async-start | bytes 1179648 | tf_op jit(solution)/shard_map/reduce_scatter | solution.py:57
  787.5 2.4 copy-start.9
  794.8 4.8 copy-start.1
  802.5 186.4 %all-reduce.14.cloned.1.call-start = ((), (), s32[]{:S(2)}) async-start(), calls=%async_computation.13 | async-start | bytes 3145728 | tf_op jit(solution)/shard_map/psum | solution.py:61
  838.8 1.1 copy-start.12
  838.8 200.4 %reduce-scatter.11.cloned.1.call-start = ((), (), s32[]{:S(2)}) async-start(), calls=%async_computation.7 | async-start | bytes 1179648 | tf_op jit(solution)/shard_map/reduce_scatter | solution.py:57
  988.9 2.4 copy-start.10
  999.5 3.0 copy-start.14
  999.5 3.2 copy-start
  1002.7 3.0 copy-start.17
  1002.7 3.1 copy-start.16
  1005.7 186.7 %all-reduce.12.cloned.1.call-start = ((), (), s32[]{:S(2)}) async-start(), calls=%async_computation.12 | async-start | bytes 3145728 | tf_op jit(solution)/shard_map/psum | solution.py:61
  1192.4 1.5 copy-start.7
  1194.0 1.6 copy-start.4
  1194.0 2.3 copy-start.5
  1194.0 2.6 copy-start.6
Sparse Core Ops, SparseCore 0:
  11.2 75.5 all-gather.8
  89.3 73.7 all-gather.10
  165.7 73.7 all-gather.12
  242.6 73.7 all-gather.14
  319.4 78.2 all-reduce.19
  400.7 33.8 reduce-scatter.4
  438.6 148.6 all-reduce.17
  600.8 33.4 reduce-scatter.6
  638.8 148.6 all-reduce.15
  802.6 33.3 reduce-scatter.8
  840.2 148.6 all-reduce.13
  1005.8 33.3 reduce-scatter.10
  1043.7 148.6 all-reduce.11
where the time goes:
time: 1220 us; the launch traced here: 1210 us
  waiting for transfers between devices  1080 us (89%)
  matrix products  47.8 us (4%)
  local copies, waits for them, and re-layouts  37.9 us (3%)
  other arithmetic  27.3 us (2%)
  between operations  14.9 us (1%)
    psum x4, waiting for transfers between devices, on_device(): row_sum, diag_sum = lax.psum((row_part, diag_part), 'prow')  592 us
    all_gather x4, waiting for transfers between devices, on_device(): lhat_class = lax.all_gather(lhat_t[k], 'prow', axis=0, tiled=True)  297 us
    reduce_scatter x4, waiting for transfers between devices, on_device(): summed = lax.psum_scatter(col_part, 'pcol', scatter_dimension=1, tiled=True)  115 us
    psum x1, waiting for transfers between devices, spread(): return lax.psum(block, axis)  70 us
  transfers between devices with their start and end apart: 13, of which 13 were waited for; matrix products, arithmetic and copies ran while one was open for 4% of the time, Pallas kernels for 0%

commit v1 on v0

v1 whole, which is shorter than its diff:
```python
import functools

import jax
import jax.numpy as jnp
from jax import lax
from jax.experimental import pallas as pl
from jax.experimental.pallas import tpu as pltpu
from jax.sharding import PartitionSpec as P

MESH = pl.DeviceIdType.MESH
NZ = 8
NX = 4
NQ = 8
F32 = jnp.float32
BF16 = jnp.bfloat16


def dev(p, q):
    return {"prow": p, "pcol": q}


def copy_to(src, dst, send, recv, device):
    return pltpu.make_async_remote_copy(
        src_ref=src, dst_ref=dst, send_sem=send, recv_sem=recv, device_id=device, device_id_type=MESH
    )


def halves(x):
    hi = x.astype(BF16)
    lo = (x - hi.astype(F32)).astype(BF16)
    return hi, lo


def dot_nn(a, b):
    return jnp.dot(a, b, preferred_element_type=F32)


def dot_nt(a, b):
    return lax.dot_general(a, b, (((1,), (1,)), ((), ())), preferred_element_type=F32)


def kernel(
    rb, root, lhat, dinv, xo, do,
    cls_out, cls_in, lrow, lsp, quad, turn, gs, gr, dloc,
    z_recv, x_recv, ag_send, cls_sem, row_sem, g_sem, t_sem, d_sem,
):
    p = lax.axis_index("prow")
    q = lax.axis_index("pcol")
    z, x = p // NX, p % NX
    r = p % NQ
    j = z // 2

    dcopy = pltpu.make_async_copy(dinv.at[:, pl.ds(pl.multiple_of(p * 32, 32), 32), :], dloc, d_sem)
    dcopy.start()

    barrier = pltpu.get_barrier_semaphore()

    def hail_z(d, c):
        pl.semaphore_signal(barrier, inc=1, device_id=dev((z + d) % NZ * NX + x, q), device_id_type=MESH)
        return c

    def hail_x(d, c):
        pl.semaphore_signal(barrier, inc=1, device_id=dev(z * NX + (x + d) % NX, q), device_id_type=MESH)
        return c

    def hail_q(d, c):
        pl.semaphore_signal(barrier, inc=1, device_id=dev(p, (q + d) % NQ), device_id_type=MESH)
        return c

    lax.fori_loop(1, NZ, hail_z, 0)
    lax.fori_loop(1, NX, hail_x, 0)
    lax.fori_loop(1, NQ, hail_q, 0)

    slot = [rb[0, 2 * r + t] == 32 + p for t in range(2)]
    for c in range(2):
        mine = rb[0, 2 * q + c]
        col = root[:, 0:128]
        for m in range(1, 4):
            col = jnp.where(mine == 32 + 8 * m + q, root[:, 128 * m : 128 * m + 128], col)
        for t in range(2):
            kept = jnp.where(slot[t], col, jnp.zeros_like(col))
            cls_out[2 * t, c] = kept[0:64]
            cls_out[2 * t + 1, c] = kept[64:128]

    pl.semaphore_wait(barrier, NZ + NX + NQ - 3)

    def class_peer(e, c):
        o = (j + e) % 4
        copy_to(
            cls_out.at[o], cls_in.at[j], cls_sem.at[0], cls_sem.at[1], dev((2 * o + z % 2) * NX + x, q)
        ).start()
        return c

    lax.fori_loop(1, 4, class_peer, 0)

    def row_peer(e, c):
        copy_to(lhat, lrow.at[q], row_sem.at[0], row_sem.at[1], dev(p, (q + e) % NQ)).start()
        return c

    lax.fori_loop(1, NQ, row_peer, 0)
    lrow[q] = lhat[...]

    def chunk_a(zz, xx):
        jj = zz // 2
        rr = zz % 2 * NX + xx
        return quad.at[:, jj // 2, pl.ds(pl.multiple_of(128 * rr + 64 * (jj % 2), 64), 64), :]

    def chunk_x(k, c):
        return lambda zz, xx: xo.at[k, c, pl.ds(pl.multiple_of(32 * (zz * NX + xx), 32), 32), :]

    def chunk_d(k):
        return lambda zz, xx: do.at[k, pl.ds(pl.multiple_of(32 * (zz * NX + xx), 32), 32), :]

    def to_x(chunk, n, zz):
        ref = chunk(zz, x)

        def one(e, c):
            copy_to(ref, ref, ag_send.at[n], x_recv.at[n], dev(z * NX + (x + e) % NX, q)).start()
            return c

        lax.fori_loop(1, NX, one, 0)

    def start_gather(chunk, n):
        ref = chunk(z, x)

        def one(i, c):
            d = (i + 4) % NZ
            d = d + (d == 0) * 4
            copy_to(ref, ref, ag_send.at[n], z_recv.at[n, d], dev((z + d) % NZ * NX + x, q)).start()
            return c

        lax.fori_loop(0, 4, one, 0)
        lax.fori_loop(5, 8, one, 0)
        to_x(chunk, n, z)

    def forward(chunk, n):
        def one(i, c):
            h = i // 2 + 1
            d = h + (i % 2) * (NZ - 2 * h)
            zz = (z + NZ - d) % NZ
            ref = chunk(zz, x)
            copy_to(ref, ref, ag_send.at[n], z_recv.at[n, d], dev(p, q)).wait_recv()
            to_x(chunk, n, zz)
            return c

        lax.fori_loop(0, NZ - 1, one, 0)

    def wait_gather(whole, n):
        copy_to(whole, whole, ag_send.at[n], x_recv.at[n], dev(p, q)).wait_recv()

    def wait_sent(whole, n):
        copy_to(whole, whole, ag_send.at[n], x_recv.at[n], dev(p, q)).wait_send()

    def wait_x(k, c, n):
        wait_gather(xo.at[k, c, pl.ds(0, 768), :], n)

    N_A = 12

    def n_x(k, c):
        return 3 * k + c

    def n_d(k):
        return 3 * k + 2

    part = cls_in.at[pl.ds(0, 3)]
    copy_to(part, part, cls_sem.at[0], cls_sem.at[1], dev(p, q)).wait_recv()
    own = cls_out[j]
    for e in range(1, 4):
        own = own + cls_in[(j + e) % 4]
    quad[:, j // 2, pl.ds(pl.multiple_of(128 * r + 64 * (j % 2), 64), 64), :] = own
    start_gather(chunk_a, N_A)

    part7 = lrow.at[pl.ds(0, 7)]
    copy_to(part7, part7, row_sem.at[0], row_sem.at[1], dev(p, q)).wait_recv()

    def split_rows(k, c):
        for o in range(NQ):
            v = lrow[o, k]
            hi, lo = halves(v)
            for h in range(2):
                lsp[k, h, 0:32, 128 * o : 128 * o + 128] = hi[:, 128 * h : 128 * h + 128]
                lsp[k, h, 32:64, 128 * o : 128 * o + 128] = lo[:, 128 * h : 128 * h + 128]
        return c

    lax.fori_loop(0, 4, split_rows, 0)
    dcopy.wait()
    forward(chunk_a, N_A)
    wait_gather(quad.at[:, :, pl.ds(0, 768), :], N_A)

    def new_x(k, c):
        both = jnp.zeros((64, 128), F32)
        small = jnp.zeros((32, 128), F32)
        for h in range(2):
            hi, lo = halves(quad[c, h])
            both = both + dot_nn(lsp[k, h], hi)
            small = small + dot_nn(lsp[k, h, 0:32], lo)
        xo[k, c, pl.ds(pl.multiple_of(32 * p, 32), 32), :] = -(both[0:32] + both[32:64] + small)
        start_gather(chunk_x(k, c), n_x(k, c))

    new_x(0, 1)
    new_x(0, 0)
    forward(chunk_x(0, 1), n_x(0, 1))
    forward(chunk_x(0, 0), n_x(0, 0))
    wait_sent(quad.at[:, :, pl.ds(0, 992), :], N_A)

    def step(k, carry):
        wait_x(k, 1, n_x(k, 1))
        wait_x(k, 0, n_x(k, 0))
        lh, ll = halves(lhat[k])
        lboth = jnp.concatenate([lh, ll], axis=0)
        for o in range(NQ):
            rows = slice(128 * o, 128 * o + 128)
            xv = jnp.concatenate([xo[k, 0, rows, :], xo[k, 1, rows, :]], axis=1)
            xh, xl = halves(xv)
            g2 = dot_nt(lboth, xh)
            gs[k, o] = g2[0:32] + g2[32:64] + dot_nt(lh, xl)

        def g_peer(e, c):
            o = (q + e) % NQ
            copy_to(gs.at[k, o], gr.at[k, q], g_sem.at[k, 0], g_sem.at[k, 1], dev(p, o)).start()
            return c

        lax.fori_loop(1, NQ, g_peer, 0)
        gr[k, q] = gs[k, q]

        @pl.when(k < 3)
        def _():
            second = rb[k + 1, 2 * q + 1] == rb[k, 2 * q + 1]
            for o in range(NQ):
                rows = slice(128 * o, 128 * o + 128)
                low = rb[k + 1, 2 * o + 1] == rb[k, 2 * o + 1]
                top = jnp.where(second, quad[1, 0, rows, :], quad[0, 0, rows, :])
                bot = jnp.where(second, quad[1, 1, rows, :], quad[0, 1, rows, :])
                quad[1, 1, rows, :] = jnp.where(low, bot, top)
                quad[1, 0, rows, :] = jnp.where(second, xo[k, 1, rows, :], xo[k, 0, rows, :])

            def t_peer(e, c):
                o = (q + e) % NQ
                copy_to(
                    quad.at[1, 0, pl.ds(pl.multiple_of(128 * o, 128), 128), :], turn.at[k, q],
                    t_sem.at[k, 0], t_sem.at[k, 1], dev(p, o),
                ).start()
                return c

            lax.fori_loop(1, NQ, t_peer, 0)
            turn[k, q] = quad[1, 0, pl.ds(pl.multiple_of(128 * q, 128), 128), :]
            new_x(k + 1, 1)

        got = gr.at[k, pl.ds(0, 7)]
        copy_to(got, got, g_sem.at[k, 0], g_sem.at[k, 1], dev(p, q)).wait_recv()
        total = gr[k, 0]
        for o in range(1, NQ):
            total = total + gr[k, o]
        do[k, pl.ds(pl.multiple_of(32 * p, 32), 32), :] = dloc[k] - total
        start_gather(chunk_d(k), n_d(k))

        @pl.when(k < 3)
        def _():
            forward(chunk_x(k + 1, 1), n_x(k + 1, 1))
            got_t = turn.at[k, pl.ds(0, 7)]
            copy_to(got_t, got_t, t_sem.at[k, 0], t_sem.at[k, 1], dev(p, q)).wait()
            for o in range(NQ):
                quad[0, 1, 128 * o : 128 * o + 128, :] = turn[k, o].T

        forward(chunk_d(k), n_d(k))
        wait_gather(do.at[k, pl.ds(0, 768), :], n_d(k))

        @pl.when(k < 3)
        def _():
            quad[0, 0] = do[k]
            new_x(k + 1, 0)
            forward(chunk_x(k + 1, 0), n_x(k + 1, 0))

        return carry

    lax.fori_loop(0, 4, step, 0)

    def finish(k, c):
        wait_sent(xo.at[k, 0, pl.ds(0, 992), :], n_x(k, 0))
        wait_sent(xo.at[k, 1, pl.ds(0, 992), :], n_x(k, 1))
        wait_sent(do.at[k, pl.ds(0, 992), :], n_d(k))
        sent = gr.at[k, pl.ds(0, 7)]
        copy_to(sent, sent, g_sem.at[k, 0], g_sem.at[k, 1], dev(p, q)).wait_send()
        return c

    lax.fori_loop(0, 4, finish, 0)
    copy_to(part, part, cls_sem.at[0], cls_sem.at[1], dev(p, q)).wait_send()
    copy_to(part7, part7, row_sem.at[0], row_sem.at[1], dev(p, q)).wait_send()


def on_device(root_cov, row_blocks, lhat_t, diag_inv):
    vmem = pl.BlockSpec(memory_space=pltpu.VMEM)
    dma = pltpu.SemaphoreType.DMA
    xs, ds = pl.pallas_call(
        kernel,
        out_shape=(
            jax.ShapeDtypeStruct((4, 2, 1024, 128), F32),
            jax.ShapeDtypeStruct((4, 1024, 128), F32),
        ),
        in_specs=[
            pl.BlockSpec(memory_space=pltpu.SMEM),
            vmem,
            vmem,
            pl.BlockSpec(memory_space=pl.ANY),
        ],
        out_specs=(vmem, vmem),
        scratch_shapes=[
            pltpu.VMEM((4, 2, 64, 128), F32),
            pltpu.VMEM((4, 2, 64, 128), F32),
            pltpu.VMEM((8, 4, 32, 256), F32),
            pltpu.VMEM((4, 2, 64, 1024), BF16),
            pltpu.VMEM((2, 2, 1024, 128), F32),
            pltpu.VMEM((3, 8, 128, 128), F32),
            pltpu.VMEM((4, 8, 32, 128), F32),
            pltpu.VMEM((4, 8, 32, 128), F32),
            pltpu.VMEM((4, 32, 128), F32),
            dma((13, 8)),
            dma((13,)),
            dma((13,)),
            dma((2,)),
            dma((2,)),
            dma((4, 2)),
            dma((3, 2)),
            dma,
        ],
        compiler_params=pltpu.CompilerParams(
            collective_id=0, has_side_effects=True, vmem_limit_bytes=48 << 20
        ),
        name="selinv",
    )(row_blocks, root_cov, lhat_t, diag_inv)
    panels = xs.transpose(0, 2, 1, 3).reshape(4, 1024, 256)
    return panels, ds


def solution(mesh):
    return jax.shard_map(
        on_device,
        mesh=mesh,
        in_specs=(P("prow", "pcol"), P(), P(None, "prow", "pcol"), P(None, None, "pcol")),
        out_specs=(P(None, None, "pcol"), P(None, None, "pcol")),
        check_vma=False,
    )
```

time: 1220 us -> 191 us (0.16); the launches traced: 1210 us -> 191 us
  waiting for transfers between devices: 1080 us -> 0 us
  Pallas kernels: 0 us -> 174 us
  matrix products: 47.8 us -> 0 us
  other arithmetic: 27.3 us -> 0 us
  local copies, waits for them, and re-layouts: 37.9 us -> 16.2 us
  between operations: 14.9 us -> 0.65 us
    psum x5 -> x0, waiting for transfers between devices: 662 us -> none  [the longest x4 592 us: on_device(): row_sum, diag_sum = lax.psum((row_part, diag_part), 'prow')]
    all_gather x4 -> x0, waiting for transfers between devices: 297 us -> none  [on_device(): lhat_class = lax.all_gather(lhat_t[k], 'prow', axis=0, tiled=True)]
    pallas_call x0 -> x1, Pallas kernels: none -> 174 us  [on_device(): pl.pallas_call(kernel, out_shape=(jax.ShapeDtypeStruct((4, 2, 1024, 128),...]
    reduce_scatter x4 -> x0, waiting for transfers between devices: 115 us -> none  [on_device(): summed = lax.psum_scatter(col_part, 'pcol', scatter_dimension=1, tiled=True)]
    dot_general x19 -> x0, matrix products: 47.8 us -> none  [the longest x4 13.3 us: on_device(): jnp.einsum('wjr,lj->wlr', lhat_owner.reshape(W, per_col, BLOCK), chosen,...]
    reshape x12 -> x0, local copies, waits for them, and re-layouts: 12.6 us -> none  [the longest x4 6.11 us: on_device(): lhat_owner.reshape(W, per_col, BLOCK)]
    another operation x7 -> x0, other arithmetic: 12.3 us -> none  [on_device(): return (jnp.stack(panels), jnp.stack(diagonal_list))]
  transfers between devices with their start and end apart: 13 -> 0, of which waited for: 13 -> 0; matrix products, arithmetic and copies ran while one was open for 4% -> 0% of each run, Pallas kernels for 0% -> 0%
where the time goes in v1:
time: 191 us
  Pallas kernels  174 us (91%)
  local copies, waits for them, and re-layouts  16.2 us (8%)
    pallas_call x1, Pallas kernels, on_device(): pl.pallas_call(kernel, out_shape=(jax.ShapeDtypeStruct((4, 2, 1024, 128),...  174 us
    unnamed x10, local copies, waits for them, and re-layouts  10.8 us
    transpose x1, local copies, waits for them, and re-layouts, on_device(): panels = xs.transpose(0, 2, 1, 3).reshape(4, 1024, 256)  5.42 us

profile of v1, /device:TPU:1, one launch (start us, length us, event | category | flops | bytes accessed | tf_op | source)
XLA Modules:
  0.0 190.9 jit_solution(9119156129873789879)
XLA Ops:
  0.6 0.0 copy-start
  0.6 1.6 copy-done
  2.2 0.0 copy-start.1
  2.2 0.9 copy-done.1
  3.2 0.0 copy-start.2
  3.2 0.9 copy-done.2
  4.1 0.0 copy-start.3
  4.1 0.7 copy-done.3
  4.8 174.0 %selinv.1 = (f32[4,2,1024,128]{3,2,1,0:T(8,128)}, f32[4,1024,128]{2,1,0:T(8,128)S(1)}) custom-call(s32[4,16]{1,0:T(4,128)S(1)} %copy-done.3, f32[128,512]{1,0:T(8,128)S(1)} %copy-done.1, f32[4,32,256]{2,1,0:T(8,128)S(1)} %copy-done.2, f32[4,1024,128]{2,1,0:T(8,128)S(1)} %copy-done), custom_call_target="tpu_custom_call" | custom-call | tf_op jit(solution)/shard_map/selinv/pallas_call | solution.py:294
  178.8 5.4 %copy.6 = f32[4,1024,2,128]{1,3,2,0:T(8,128)} copy(f32[4,1024,2,128]{3,1,2,0:T(8,128)} %bitcast.3) | data formatting | bytes 8388608 | tf_op jit(solution)/shard_map/transpose | solution.py:331
  184.2 5.4 %copy.7 = f32[4,1024,256]{2,1,0:T(8,128)} copy(f32[4,1024,256]{1,2,0:T(8,128)} %bitcast.2) | data formatting | bytes 8388608
  189.6 1.3 copy.9
Async XLA Ops:
  0.6 1.6 copy-start
  2.2 0.9 copy-start.1
  3.2 0.9 copy-start.2
  4.1 0.7 copy-start.3

commit v2 on v0

v2 whole, which is shorter than its diff:
```python
import jax
import jax.numpy as jnp
from jax import lax
from jax.experimental import pallas as pl
from jax.experimental.pallas import tpu as pltpu
from jax.sharding import PartitionSpec as P

MESH = pl.DeviceIdType.MESH
NZ = 8
NX = 4
NQ = 8
F32 = jnp.float32
BF16 = jnp.bfloat16


def dev(p, q):
    return {"prow": p, "pcol": q}


def copy_to(src, dst, send, recv, device):
    return pltpu.make_async_remote_copy(
        src_ref=src, dst_ref=dst, send_sem=send, recv_sem=recv, device_id=device, device_id_type=MESH
    )


def halves(x):
    hi = x.astype(BF16)
    lo = (x - hi.astype(F32)).astype(BF16)
    return hi, lo


def stacked(x):
    return jnp.concatenate(halves(x), axis=0)


def dot_nn(a, b):
    return jnp.dot(a, b, preferred_element_type=F32)


def dot_nt(a, b):
    return lax.dot_general(a, b, (((1,), (1,)), ((), ())), preferred_element_type=F32)


def rows(i, n):
    return pl.ds(pl.multiple_of(i * n, n), n)


def kernel(
    rb, root_h, lhat_h, dinv_h, out_x, out_d,
    root, lhat, dblk, dturn, cls_out, cls_in, lrow0, lrow, lx, az, xp, xr, bsel, xsel,
    lc, lsp, ltt, xo, ed, do, turn, gs, gr,
    in_sem, cls_sem, row0_sem, row_sem, lx_sem, az_sem, xr_sem, b_sem, lc_sem, g_sem, t_sem,
    z_recv, x_recv, c_recv, ag_send, o_sem,
):
    p = lax.axis_index("prow")
    q = lax.axis_index("pcol")
    z, x = p // NX, p % NX
    me = dev(p, q)
    par, quarter = z % 2, z // 2

    loads = [
        pltpu.make_async_copy(root_h, root, in_sem.at[0]),
        pltpu.make_async_copy(lhat_h, lhat, in_sem.at[1]),
        pltpu.make_async_copy(dinv_h.at[:, rows(z, 128), :], dblk, in_sem.at[2]),
    ]
    for load in loads:
        load.start()

    def to_z(d):
        return dev((z + d) % NZ * NX + x, q)

    def to_x(e):
        return dev(z * NX + (x + e) % NX, q)

    def to_q(e):
        return dev(p, (q + e) % NQ)

    def loop(a, b, body):
        def run(i, c):
            body(i)
            return c

        lax.fori_loop(a, b, run, 0)

    barrier = pltpu.get_barrier_semaphore()
    loop(1, NZ, lambda d: pl.semaphore_signal(barrier, inc=1, device_id=to_z(d), device_id_type=MESH))
    loop(1, NX, lambda e: pl.semaphore_signal(barrier, inc=1, device_id=to_x(e), device_id_type=MESH))
    loop(1, NQ, lambda e: pl.semaphore_signal(barrier, inc=1, device_id=to_q(e), device_id_type=MESH))

    def got(ref, recv):
        copy_to(ref, ref, recv, recv, me).wait_recv()

    def sent(ref, send):
        copy_to(ref, ref, send, send, me).wait_send()

    loads[0].wait()
    home = par * NX + x
    slot = [rb[0, 2 * home + t] == 32 + p for t in range(2)]
    for c in range(2):
        mine = rb[0, 2 * q + c]
        col = root[:, 0:128]
        for m in range(1, 4):
            col = jnp.where(mine == 32 + 8 * m + q, root[:, 128 * m : 128 * m + 128], col)
        for t in range(2):
            kept = jnp.where(slot[t], col, jnp.zeros_like(col))
            cls_out[2 * t, c] = kept[0:64]
            cls_out[2 * t + 1, c] = kept[64:128]
    loads[1].wait()
    pl.semaphore_wait(barrier, NZ + NX + NQ - 3)

    def class_peer(e):
        o = (quarter + e) % 4
        copy_to(
            cls_out.at[o], cls_in.at[quarter], cls_sem.at[0], cls_sem.at[1], dev((2 * o + par) * NX + x, q)
        ).start()

    loop(1, 4, class_peer)
    qh, qx = q // NX, q % NX
    loop(1, NQ, lambda e: copy_to(lhat.at[0], lrow0.at[qh, qx], row0_sem.at[0], row0_sem.at[1], to_q(e)).start())
    loop(
        1, NQ,
        lambda e: copy_to(lhat.at[pl.ds(1, 3)], lrow.at[q], row_sem.at[0], row_sem.at[1], to_q(e)).start(),
    )
    lrow0[qh, qx] = lhat[0]
    lrow[q] = lhat[1:4]
    for k in range(4):
        lc[k, z] = lhat[k]

    def send_lc(k):
        loop(1, NZ, lambda d: copy_to(lhat.at[k], lc.at[k, z], lc_sem.at[k, 0], lc_sem.at[k, 1], to_z(d)).start())

    def order(i):
        h = i // 2 + 1
        return h + (i % 2) * (NZ - 2 * h)

    got(cls_in.at[pl.ds(0, 3)], cls_sem.at[1])
    own = cls_out[quarter]
    for e in range(1, 4):
        own = own + cls_in[(quarter + e) % 4]
    az_own = az.at[:, par, rows(quarter, 64), :]
    az_own[...] = own
    loop(0, NZ - 1, lambda i: copy_to(az_own, az_own, az_sem.at[0], az_sem.at[1], to_z(order(6 - i))).start())
    send_lc(0)

    got(lrow0.at[0, pl.ds(0, 7)], row0_sem.at[1])

    def lx_peer(e):
        copy_to(lrow0.at[:, (x + e) % NX], lx.at[x], lx_sem.at[0], lx_sem.at[1], to_x(e)).start()

    loop(1, NX, lx_peer)
    lx[x] = lrow0[:, x]

    loads[2].wait()

    def turn_dinv(k):
        dturn[k] = dblk[k].T

    loop(0, 4, turn_dinv)
    got(lrow.at[pl.ds(0, 7)], row_sem.at[1])

    def prepare(k):
        for o in range(NQ):
            for h in range(2):
                v = lrow[o, k, :, 128 * h : 128 * h + 128]
                hi, lo = halves(v)
                lsp[k, h, 0:32, 128 * o : 128 * o + 128] = hi
                lsp[k, h, 32:64, 128 * o : 128 * o + 128] = lo
                ltt[k, h, 128 * o : 128 * o + 128, :] = jnp.concatenate(halves(v.T), axis=1)

    loop(0, 3, prepare)

    def chunk_x(k, c):
        return lambda zz, xx: xo.at[k, c, rows(zz * NX + xx, 32), :]

    def chunk_d(k):
        return lambda zz, xx: ed.at[k, rows(zz * NX + xx, 32), :]

    def n_x(k, c):
        return 3 * k + c

    def n_d(k):
        return 3 * k + 2

    def start_gather(chunk, n):
        ref = chunk(z, x)
        loop(1, NX, lambda e: copy_to(ref, ref, ag_send.at[n], c_recv.at[n], to_x(e)).start())

        def one(i):
            d = order(6 - i)
            copy_to(ref, ref, ag_send.at[n], z_recv.at[n, d], to_z(d)).start()

        loop(0, NZ - 1, one)

    def forward(chunk, n):
        def one(i):
            d = order(i)
            ref = chunk((z + NZ - d) % NZ, x)
            got(ref, z_recv.at[n, d])
            loop(1, NX, lambda e: copy_to(ref, ref, ag_send.at[n], x_recv.at[n], to_x(e)).start())

        loop(0, NZ - 1, one)

    def put_x(k, c, value):
        xo[k, c, rows(p, 32), :] = value
        start_gather(chunk_x(k, c), n_x(k, c))

    got(lx.at[pl.ds(0, 3)], lx_sem.at[1])
    got(az.at[:, :, pl.ds(0, 224), :], az_sem.at[1])
    lefts = [halves(jnp.concatenate([lx[e, h] for e in range(NX)], axis=0)) for h in range(2)]
    for c in range(2):
        total = jnp.zeros((128, 128), F32)
        for h in range(2):
            hi, lo = halves(az[c, h])
            total = total + dot_nn(lefts[h][0], hi) + dot_nn(lefts[h][1], hi) + dot_nn(lefts[h][0], lo)
        for e in range(NX):
            xp[e, c] = total[32 * e : 32 * e + 32]

    def xp_peer(e):
        copy_to(xp.at[(x + e) % NX], xr.at[x], xr_sem.at[0], xr_sem.at[1], to_x(e)).start()

    loop(1, NX, xp_peer)
    xr[x] = xp[x]

    second = rb[1, 2 * q + 1] == rb[0, 2 * q + 1]
    for h in range(2):
        o = x + NX * h
        low = rb[1, 2 * o + 1] == rb[0, 2 * o + 1]
        top = jnp.where(second, az[1, h, 0:128], az[0, h, 0:128])
        bot = jnp.where(second, az[1, h, 128:256], az[0, h, 128:256])
        bsel[h, x] = jnp.where(low, bot, top)
    b_own = bsel.at[:, x]
    loop(1, NX, lambda e: copy_to(b_own, b_own, b_sem.at[0], b_sem.at[1], to_x(e)).start())

    got(xr.at[pl.ds(0, 3)], xr_sem.at[1])
    first = -(xr[0] + xr[1] + xr[2] + xr[3])
    put_x(0, 0, first[0])
    put_x(0, 1, first[1])

    def step(k, carry):
        got(xo.at[k, 1, pl.ds(0, 96), :], c_recv.at[n_x(k, 1)])
        got(lc.at[k, pl.ds(0, 7)], lc_sem.at[k, 1])
        got(xo.at[k, 0, pl.ds(0, 96), :], c_recv.at[n_x(k, 0)])
        xh, xl = halves(jnp.concatenate([xo[k, 0, rows(z, 128), :], xo[k, 1, rows(z, 128), :]], axis=1))
        ch, cl = halves(lc[k].reshape(256, 256))
        part = dot_nt(ch, xh) + dot_nt(cl, xh) + dot_nt(ch, xl)
        gs[k] = part.reshape(NQ, 32, 128)

        def g_peer(e):
            copy_to(gs.at[k, (q + e) % NQ], gr.at[k, q], g_sem.at[k, 0], g_sem.at[k, 1], to_q(e)).start()

        loop(1, NQ, g_peer)
        gr[k, q] = gs[k, q]
        forward(chunk_x(k, 1), n_x(k, 1))
        forward(chunk_x(k, 0), n_x(k, 0))

        got(gr.at[k, pl.ds(0, 7)], g_sem.at[k, 1])
        total = gr[k, 0]
        for o in range(1, NQ):
            total = total + gr[k, o]
        ed[k, rows(p, 32), :] = dturn[k, rows(x, 32), :] - total
        start_gather(chunk_d(k), n_d(k))

        got(xo.at[k, 1, pl.ds(0, 672), :], x_recv.at[n_x(k, 1)])
        got(xo.at[k, 0, pl.ds(0, 672), :], x_recv.at[n_x(k, 0)])

        @pl.when(k < 3)
        def _():
            pick = rb[k + 1, 2 * q + 1] == rb[k, 2 * q + 1]

            @pl.when(k > 0)
            def _():
                for o in range(NQ):
                    lower = rb[k + 1, 2 * o + 1] == rb[k, 2 * o + 1]
                    span = slice(128 * o, 128 * o + 128)
                    upper_part = jnp.where(pick, xsel[span, :], do[k - 1, span, :])
                    lower_part = jnp.where(pick, bsel[o // NX, o % NX], turn[k - 1, o].T)
                    bsel[o // NX, o % NX] = jnp.where(lower, lower_part, upper_part)

            xsel[...] = jnp.where(pick, xo[k, 1], xo[k, 0])

            def t_peer(e):
                copy_to(
                    xsel.at[rows((q + e) % NQ, 128), :], turn.at[k, q], t_sem.at[k, 0], t_sem.at[k, 1], to_q(e)
                ).start()

            loop(1, NQ, t_peer)
            turn[k, q] = xsel[rows(q, 128), :]

        forward(chunk_d(k), n_d(k))
        for c in range(2):
            pltpu.make_async_copy(
                xo.at[k, c], out_x.at[k, :, pl.ds(128 * c, 128)], o_sem.at[k, c]
            ).start()

        @pl.when(k < 3)
        def _():
            send_lc(k + 1)

            @pl.when(k == 0)
            def _():
                got(bsel.at[:, pl.ds(0, 3)], b_sem.at[1])
                sent(bsel.at[:, pl.ds(0, 3)], b_sem.at[0])

            both = jnp.zeros((64, 128), F32)
            small = jnp.zeros((32, 128), F32)
            for h in range(2):
                hi, lo = halves(xsel[...] if h == 0 else bsel[...].reshape(1024, 128))
                both = both + dot_nn(lsp[k, h], hi)
                small = small + dot_nn(lsp[k, h, 0:32], lo)
            put_x(k + 1, 1, -(both[0:32] + both[32:64] + small))
            got(turn.at[k, pl.ds(0, 7)], t_sem.at[k, 1])
            sent(turn.at[k, pl.ds(0, 7)], t_sem.at[k, 0])

        got(ed.at[k, pl.ds(0, 96), :], c_recv.at[n_d(k)])
        got(ed.at[k, pl.ds(0, 672), :], x_recv.at[n_d(k)])

        @pl.when(k < 3)
        def _():
            acc = jnp.zeros((256, 64), F32)
            for o in range(0, NQ, 2):
                wide = slice(128 * o, 128 * o + 256)
                t = jnp.concatenate([turn[k, o], turn[k, o + 1]], axis=1)
                e = jnp.concatenate(
                    [ed[k, 128 * o : 128 * o + 128, :], ed[k, 128 * o + 128 : 128 * o + 256, :]], axis=1
                )
                acc = acc + dot_nn(stacked(t), ltt[k, 1, wide, :]) + dot_nn(stacked(e), ltt[k, 0, wide, :])
            new = acc[0:128, 0:32] + acc[0:128, 32:64] + acc[128:256, 0:32]
            put_x(k + 1, 0, -new.T)

        for o in range(NQ):
            do[k, 128 * o : 128 * o + 128, :] = ed[k, 128 * o : 128 * o + 128, :].T
        pltpu.make_async_copy(do.at[k], out_d.at[k], o_sem.at[k, 2]).start()
        return carry

    lax.fori_loop(0, 4, step, 0)

    def finish(k):
        for c in range(2):
            sent(xo.at[k, c, pl.ds(0, 992), :], ag_send.at[n_x(k, c)])
            pltpu.make_async_copy(xo.at[k, c], out_x.at[k, :, pl.ds(128 * c, 128)], o_sem.at[k, c]).wait()
        sent(ed.at[k, pl.ds(0, 992), :], ag_send.at[n_d(k)])
        sent(gr.at[k, pl.ds(0, 7)], g_sem.at[k, 0])
        sent(lc.at[k, pl.ds(0, 7)], lc_sem.at[k, 0])
        pltpu.make_async_copy(do.at[k], out_d.at[k], o_sem.at[k, 2]).wait()

    loop(0, 4, finish)
    sent(cls_in.at[pl.ds(0, 3)], cls_sem.at[0])
    sent(lrow0.at[0, pl.ds(0, 7)], row0_sem.at[0])
    sent(lrow.at[pl.ds(0, 7)], row_sem.at[0])
    sent(lx.at[pl.ds(0, 3)], lx_sem.at[0])
    sent(az.at[:, :, pl.ds(0, 224), :], az_sem.at[0])
    sent(xr.at[pl.ds(0, 3)], xr_sem.at[0])


def on_device(root_cov, row_blocks, lhat_t, diag_inv):
    anywhere = pl.BlockSpec(memory_space=pl.ANY)
    dma = pltpu.SemaphoreType.DMA
    vmem = pltpu.VMEM
    return pl.pallas_call(
        kernel,
        out_shape=(
            jax.ShapeDtypeStruct((4, 1024, 256), F32),
            jax.ShapeDtypeStruct((4, 1024, 128), F32),
        ),
        in_specs=[pl.BlockSpec(memory_space=pltpu.SMEM), anywhere, anywhere, anywhere],
        out_specs=(anywhere, anywhere),
        scratch_shapes=[
            vmem((128, 512), F32),
            vmem((4, 32, 256), F32),
            vmem((4, 128, 128), F32),
            vmem((4, 128, 128), F32),
            vmem((4, 2, 64, 128), F32),
            vmem((4, 2, 64, 128), F32),
            vmem((2, 8, 32, 256), F32),
            vmem((8, 3, 32, 256), F32),
            vmem((4, 2, 32, 256), F32),
            vmem((2, 2, 256, 128), F32),
            vmem((4, 2, 32, 128), F32),
            vmem((4, 2, 32, 128), F32),
            vmem((2, 4, 128, 128), F32),
            vmem((1024, 128), F32),
            vmem((4, 8, 32, 256), F32),
            vmem((3, 2, 64, 1024), BF16),
            vmem((3, 2, 1024, 64), BF16),
            vmem((4, 2, 1024, 128), F32),
            vmem((4, 1024, 128), F32),
            vmem((4, 1024, 128), F32),
            vmem((3, 8, 128, 128), F32),
            vmem((4, 8, 32, 128), F32),
            vmem((4, 8, 32, 128), F32),
            dma((3,)),
            dma((2,)),
            dma((2,)),
            dma((2,)),
            dma((2,)),
            dma((2,)),
            dma((2,)),
            dma((2,)),
            dma((4, 2)),
            dma((4, 2)),
            dma((3, 2)),
            dma((12, 8)),
            dma((12,)),
            dma((12,)),
            dma((12,)),
            dma((4, 3)),
        ],
        compiler_params=pltpu.CompilerParams(
            collective_id=0, has_side_effects=True, vmem_limit_bytes=60 << 20
        ),
        name="selinv",
    )(row_blocks, root_cov, lhat_t, diag_inv)


def solution(mesh):
    return jax.shard_map(
        on_device,
        mesh=mesh,
        in_specs=(P("prow", "pcol"), P(), P(None, "prow", "pcol"), P(None, None, "pcol")),
        out_specs=(P(None, None, "pcol"), P(None, None, "pcol")),
        check_vma=False,
    )
```

time: 1220 us -> 143 us (0.12)
  waiting for transfers between devices: 1080 us -> 0 us
  Pallas kernels: 0 us -> 134 us
  matrix products: 47.8 us -> 0 us
  local copies, waits for them, and re-layouts: 37.9 us -> 6.04 us
  other arithmetic: 27.3 us -> 0 us
  between operations: 14.9 us -> 0.65 us
    psum x5 -> x0, waiting for transfers between devices: 662 us -> none  [the longest x4 592 us: on_device(): row_sum, diag_sum = lax.psum((row_part, diag_part), 'prow')]
    all_gather x4 -> x0, waiting for transfers between devices: 297 us -> none  [on_device(): lhat_class = lax.all_gather(lhat_t[k], 'prow', axis=0, tiled=True)]
    pallas_call x0 -> x1, Pallas kernels: none -> 134 us  [on_device(): pl.pallas_call(kernel, out_shape=(jax.ShapeDtypeStruct((4, 1024, 256), F3...]
    reduce_scatter x4 -> x0, waiting for transfers between devices: 115 us -> none  [on_device(): summed = lax.psum_scatter(col_part, 'pcol', scatter_dimension=1, tiled=True)]
    dot_general x19 -> x0, matrix products: 47.8 us -> none  [the longest x4 13.3 us: on_device(): jnp.einsum('wjr,lj->wlr', lhat_owner.reshape(W, per_col, BLOCK), chosen,...]
    reshape x12 -> x0, local copies, waits for them, and re-layouts: 12.6 us -> none  [the longest x4 6.11 us: on_device(): lhat_owner.reshape(W, per_col, BLOCK)]
    another operation x7 -> x0, other arithmetic: 12.3 us -> none  [on_device(): return (jnp.stack(panels), jnp.stack(diagonal_list))]
  transfers between devices with their start and end apart: 13 -> 0, of which waited for: 13 -> 0; matrix products, arithmetic and copies ran while one was open for 4% -> 0% of each run, Pallas kernels for 0% -> 0%
where the time goes in v2:
time: 143 us; the launch traced here: 141 us
  Pallas kernels  134 us (94%)
  local copies, waits for them, and re-layouts  6.04 us (4%)
    pallas_call x1, Pallas kernels, on_device(): pl.pallas_call(kernel, out_shape=(jax.ShapeDtypeStruct((4, 1024, 256), F3...  134 us
    unnamed x4, local copies, waits for them, and re-layouts  6.04 us

profile of v2, /device:TPU:1, one launch (start us, length us, event | category | flops | bytes accessed | tf_op | source)
XLA Modules:
  0.0 140.7 jit_solution(11659523217561897224)
XLA Ops:
  0.6 134.0 %selinv.1 = (f32[4,1024,256]{2,1,0:T(8,128)}, f32[4,1024,128]{2,1,0:T(8,128)}) custom-call(s32[4,16]{1,0:T(4,128)} %rb.1, f32[128,512]{1,0:T(8,128)} %root_h.1, f32[4,32,256]{2,1,0:T(8,128)} %lhat_h.1, f32[4,1024,128]{2,1,0:T(8,128)} %dinv_h.1), custom_call_target="tpu_custom_call" | custom-call | tf_op jit(solution)/shard_map/selinv/pallas_call | solution.py:359
  134.7 0.0 copy-start
  134.7 4.7 %copy.8 = f32[4,1024,256]{2,1,0:T(8,128)} copy(f32[4,1024,256]{2,1,0:T(8,128)} %get-tuple-element.4) | data formatting | bytes 8388608
  139.4 0.0 copy-done
  139.4 1.3 copy.9
Async XLA Ops:
  134.7 4.7 %copy-start = (f32[4,1024,128]{2,1,0:T(8,128)S(1)}, f32[4,1024,128]{2,1,0:T(8,128)}, u32[]{:S(2)}) copy-start(f32[4,1024,128]{2,1,0:T(8,128)} %get-tuple-element.5) | copy-start | bytes 6291460

commit v3 on v2

v3 whole, which is shorter than its diff:
```python
import jax
import jax.numpy as jnp
from jax import lax
from jax.experimental import pallas as pl
from jax.experimental.pallas import tpu as pltpu
from jax.sharding import PartitionSpec as P

MESH = pl.DeviceIdType.MESH
NZ = 8
NX = 4
NQ = 8
F32 = jnp.float32
BF16 = jnp.bfloat16
KEEP = (32, 32, 32)
EARLY = 4


def dev(p, q):
    return {"prow": p, "pcol": q}


def copy_to(src, dst, send, recv, device):
    return pltpu.make_async_remote_copy(
        src_ref=src, dst_ref=dst, send_sem=send, recv_sem=recv, device_id=device, device_id_type=MESH
    )


def halves(x):
    hi = x.astype(BF16)
    lo = (x - hi.astype(F32)).astype(BF16)
    return hi, lo


def stacked(x):
    return jnp.concatenate(halves(x), axis=0)


def dot_nn(a, b):
    return jnp.dot(a, b, preferred_element_type=F32)


def dot_nt(a, b):
    return lax.dot_general(a, b, (((1,), (1,)), ((), ())), preferred_element_type=F32)


def rows(i, n):
    return pl.ds(pl.multiple_of(i * n, n), n)


def kernel(
    rb, root_h, lhat_h, dinv_h, out_x, out_d,
    root, lhat, dblk, dturn, cls, lrow0, lrow, lx, az, xp, xr, bsel, xsel,
    lc, lsp, ltt, xo, ed, do, turn, gs, gr, held, tall,
    in_sem, cls_sem, row0_sem, row_sem, lx_sem, xr_sem, b_sem, lc_send, lc_recv, g_sem, t_sem,
    z_recv, x_recv, c_recv, b_recv, ag_send, o_sem,
):
    p = lax.axis_index("prow")
    q = lax.axis_index("pcol")
    z, x = p // NX, p % NX
    me = dev(p, q)
    par, quarter = z % 2, z // 2

    loads = [
        pltpu.make_async_copy(root_h, root, in_sem.at[0]),
        pltpu.make_async_copy(lhat_h, lhat, in_sem.at[1]),
        pltpu.make_async_copy(dinv_h.at[:, rows(z, 128), :], dblk, in_sem.at[2]),
    ]
    for load in loads:
        load.start()

    def to_z(d):
        return dev((z + d) % NZ * NX + x, q)

    def to_x(e):
        return dev(z * NX + (x + e) % NX, q)

    def to_q(e):
        return dev(p, (q + e) % NQ)

    def loop(a, b, body):
        def run(i, c):
            body(i)
            return c

        lax.fori_loop(a, b, run, 0)

    barrier = pltpu.get_barrier_semaphore()
    loop(1, NZ, lambda d: pl.semaphore_signal(barrier, inc=1, device_id=to_z(d), device_id_type=MESH))
    loop(1, NX, lambda e: pl.semaphore_signal(barrier, inc=1, device_id=to_x(e), device_id_type=MESH))
    loop(1, NQ, lambda e: pl.semaphore_signal(barrier, inc=1, device_id=to_q(e), device_id_type=MESH))

    loop(
        1, NX,
        lambda e: pl.semaphore_signal(
            barrier, inc=1, device_id=dev((2 * quarter + 1 - par) * NX + (x + e) % NX, q), device_id_type=MESH
        ),
    )

    def got(ref, recv):
        copy_to(ref, ref, recv, recv, me).wait_recv()

    def sent(ref, send):
        copy_to(ref, ref, send, send, me).wait_send()

    loads[0].wait()
    g = par * NX + x
    for c in range(2):
        mine = rb[0, 2 * q + c]
        col = root[:, 0:128]
        for m in range(1, 4):
            col = jnp.where(mine == 32 + 8 * m + q, root[:, 128 * m : 128 * m + 128], col)
        cls[quarter, c] = col
    loads[1].wait()
    pl.semaphore_wait(barrier, NZ + NX + NQ)

    def class_peer(e):
        ref = cls.at[quarter]
        copy_to(ref, ref, cls_sem.at[0], cls_sem.at[1], to_z(2 * e)).start()

    class_peer(2)
    class_peer(1)
    class_peer(3)
    loop(1, NQ, lambda e: copy_to(lhat.at[0], lrow0.at[q], row0_sem.at[0], row0_sem.at[1], to_q(e)).start())
    loop(
        1, NQ,
        lambda e: copy_to(lhat.at[pl.ds(1, 3)], lrow.at[q], row_sem.at[0], row_sem.at[1], to_q(e)).start(),
    )
    lrow0[q] = lhat[0]
    lrow[q] = lhat[1:4]
    for k in range(4):
        lc[k, z] = lhat[k]

    def lc_hop(k, far):
        for side, d in ((0, 1), (1, NZ - 1)):
            if far == 3 and side == 1:
                continue
            ref = lc.at[k, (z + NZ - far * d) % NZ]
            if far > 0:
                got(ref, lc_recv.at[k, side, far - 1])
            copy_to(ref, ref, lc_send.at[k], lc_recv.at[k, side, far], to_z(d)).start()

    def got_lc(k):
        got(lc.at[k, 0], lc_recv.at[k, 1, 2])
        got(lc.at[k, 0], lc_recv.at[k, 0, 3])

    def order(i):
        h = i // 2 + 1
        return h + (i % 2) * (NZ - 2 * h)

    got(lrow0.at[pl.ds(0, 7)], row0_sem.at[1])

    def to_group(e, body):
        o = (g + e) % NQ
        body(o, dev((2 * quarter + o // NX) * NX + o % NX, q))

    def lx_peer(e):
        to_group(
            e, lambda o, d: copy_to(lrow0.at[o], lx.at[g], lx_sem.at[0], lx_sem.at[1], d).start()
        )

    loop(1, NQ, lx_peer)
    lx[g] = lrow0[g]
    lc_hop(0, 0)

    def turn_dinv(k):
        dturn[k] = dblk[k].T


    def prepare(k):
        for o in range(NQ):
            for h in range(2):
                hi, lo = halves(lrow[o, k, :, 128 * h : 128 * h + 128])
                lsp[k, h, 0:32, 128 * o : 128 * o + 128] = hi
                lsp[k, h, 32:64, 128 * o : 128 * o + 128] = lo

    def prepare_t(k):
        for o in range(NQ):
            for h in range(2):
                v = lrow[o, k, :, 128 * h : 128 * h + 128]
                ltt[k, h, 128 * o : 128 * o + 128, :] = jnp.concatenate(halves(v.T), axis=1)

    def buf_of(k, c):
        return (xo.at[k, c], 3 * k + c, KEEP[c]) if c < 2 else (ed.at[k], 3 * k + 2, KEEP[2])

    def start_gather(k, c):
        buf, n, keep = buf_of(k, c)
        ref = buf.at[z, x]
        loop(1, NX, lambda e: copy_to(ref, ref, ag_send.at[n], c_recv.at[n], to_x(e)).start())
        top = buf.at[z, x, pl.ds(0, keep), :]

        def one(i):
            d = order(6 - i)
            copy_to(top, top, ag_send.at[n], z_recv.at[n, d], to_z(d)).start()

        loop(0, NZ - 1, one)

    def got_near(k, c):
        buf, n, keep = buf_of(k, c)
        got(buf.at[0, pl.ds(0, 3)], c_recv.at[n])

    def second_part(k, c):
        buf, n, keep = buf_of(k, c)
        if keep < 32:
            ref = buf.at[z, :, pl.ds(keep, 32 - keep), :]
            loop(
                0, NZ - 1,
                lambda i: copy_to(ref, ref, ag_send.at[n], b_recv.at[n], to_z(order(6 - i))).start(),
            )

    def forward(k, c, first, last):
        buf, n, keep = buf_of(k, c)

        def one(i):
            d = order(i)
            ref = buf.at[(z + NZ - d) % NZ, x, pl.ds(0, keep), :]
            got(ref, z_recv.at[n, d])
            loop(1, NX, lambda e: copy_to(ref, ref, ag_send.at[n], x_recv.at[n], to_x(e)).start())

        loop(first, last, one)

    def got_all(k, c):
        buf, n, keep = buf_of(k, c)
        got(buf.at[pl.ds(0, 7), pl.ds(0, 3), pl.ds(0, keep), :], x_recv.at[n])
        if keep < 32:
            got(buf.at[pl.ds(0, 7), :, pl.ds(keep, 32 - keep), :], b_recv.at[n])

    def put_x(k, c, value):
        xo[k, c, z, x] = value
        start_gather(k, c)

    got(lx.at[pl.ds(0, 7)], lx_sem.at[1])
    left, left_low = halves(lx[...].reshape(256, 256))
    got(cls.at[pl.ds(0, 3)], cls_sem.at[1])
    lc_hop(0, 1)
    for c in range(2):
        for t in range(2):
            want = rb[0, 2 * g + t]
            blk = cls[0, c]
            for o in range(1, 4):
                blk = jnp.where(want == 32 + 8 * o + g, cls[o, c], blk)
            az[c, 128 * t : 128 * t + 128, :] = blk
        hi, lo = halves(az[c])
        total = dot_nn(left, hi) + dot_nn(left_low, hi) + dot_nn(left, lo)
        xp[:, c] = total.reshape(NQ, 32, 128)

    def xp_peer(e):
        to_group(e, lambda o, d: copy_to(xp.at[o], xr.at[g], xr_sem.at[0], xr_sem.at[1], d).start())

    loop(1, NQ, xp_peer)
    xr[g] = xp[g]

    second = rb[1, 2 * q + 1] == rb[0, 2 * q + 1]
    low = rb[1, 2 * g + 1] == rb[0, 2 * g + 1]
    top = jnp.where(second, az[1, 0:128], az[0, 0:128])
    bot = jnp.where(second, az[1, 128:256], az[0, 128:256])
    bsel[g] = jnp.where(low, bot, top)
    b_own = bsel.at[g]

    def b_peer(e):
        to_group(e, lambda o, d: copy_to(b_own, b_own, b_sem.at[0], b_sem.at[1], d).start())

    loads[2].wait()
    loop(0, 4, turn_dinv)
    got(lrow.at[pl.ds(0, 7)], row_sem.at[1])
    prepare(0)
    prepare_t(0)
    lc_hop(0, 2)
    got(xr.at[pl.ds(0, 7)], xr_sem.at[1])
    first = -xr[0]
    for o in range(1, NQ):
        first = first - xr[o]
    lc_hop(0, 3)
    put_x(0, 0, first[0])
    put_x(0, 1, first[1])
    loop(1, NQ, b_peer)

    def times_split(left_rows, value):
        hi, lo = halves(value)
        both = dot_nn(left_rows[...], hi)
        return both[0:32] + both[32:64] + dot_nn(left_rows[0:32], lo)

    def times_turned(right, lefts):
        acc = jnp.zeros((256, 64), F32)
        for i, v in enumerate(lefts):
            acc = acc + dot_nn(stacked(v), right[256 * i : 256 * i + 256, :])
        return acc[0:128, 0:32] + acc[0:128, 32:64] + acc[128:256, 0:32]

    def step(k, carry):
        if KEEP[1] == 32:
            got_near(k, 1)
        else:

            @pl.when(k == 0)
            def _():
                got_near(k, 1)

        got_near(k, 0)
        got_lc(k)
        xh, xl = halves(
            jnp.concatenate([xo[k, 0, z].reshape(128, 128), xo[k, 1, z].reshape(128, 128)], axis=1)
        )
        ch, cl = halves(lc[k].reshape(256, 256))
        part = dot_nt(ch, xh) + dot_nt(cl, xh) + dot_nt(ch, xl)
        gs[k] = part.reshape(NQ, 32, 128)

        def g_peer(e):
            copy_to(gs.at[k, (q + e) % NQ], gr.at[k, q], g_sem.at[k, 0], g_sem.at[k, 1], to_q(e)).start()

        loop(1, NQ, g_peer)
        gr[k, q] = gs[k, q]
        second_part(k, 0)

        @pl.when(k == 0)
        def _():
            second_part(k, 1)
            forward(k, 1, 0, 7)

        forward(k, 0, 0, 7)

        @pl.when(k < 3)
        def _():
            lc_hop(k + 1, 0)

        @pl.when(k == 0)
        def _():
            got(bsel.at[pl.ds(0, 7)], b_sem.at[1])
            sent(bsel.at[pl.ds(0, 7)], b_sem.at[0])
            held[...] = times_split(lsp.at[0, 1], bsel[...].reshape(1024, 128))

        got(gr.at[k, pl.ds(0, 7)], g_sem.at[k, 1])
        total = gr[k, 0]
        for o in range(1, NQ):
            total = total + gr[k, o]
        ed[k, z, x] = dturn[k, rows(x, 32), :] - total
        start_gather(k, 2)
        forward(k, 2, 0, EARLY)
        if KEEP[2] < 32:
            got_near(k, 2)
            second_part(k, 2)

        @pl.when(k < 3)
        def _():
            lc_hop(k + 1, 1)

        got_all(k, 1)
        got_all(k, 0)

        @pl.when(k < 3)
        def _():
            pick = rb[k + 1, 2 * q + 1] == rb[k, 2 * q + 1]
            xsel[...] = jnp.where(pick, xo[k, 1].reshape(1024, 128), xo[k, 0].reshape(1024, 128))

            def t_peer(e):
                copy_to(
                    xsel.at[rows((q + e) % NQ, 128), :], turn.at[k, q], t_sem.at[k, 0], t_sem.at[k, 1], to_q(e)
                ).start()

            loop(1, NQ, t_peer)
            turn[k, q] = xsel[rows(q, 128), :]
            put_x(k + 1, 1, -(held[...] + times_split(lsp.at[k, 0], xsel[...])))

        forward(k, 2, EARLY, 7)
        for c in range(2):
            pltpu.make_async_copy(
                xo.at[k, c], out_x.at[k, :, :, :, pl.ds(128 * c, 128)], o_sem.at[k, c]
            ).start()

        @pl.when(k < 2)
        def _():
            prepare(k + 1)
            prepare_t(k + 1)

        @pl.when(k < 3)
        def _():
            lc_hop(k + 1, 2)
            got(turn.at[k, pl.ds(0, 7)], t_sem.at[k, 1])
            sent(turn.at[k, pl.ds(0, 7)], t_sem.at[k, 0])
            tall[...] = times_turned(
                ltt.at[k, 1], [jnp.concatenate([turn[k, o], turn[k, o + 1]], axis=1) for o in range(0, NQ, 2)]
            )
            lc_hop(k + 1, 3)
            if KEEP[1] < 32:
                got_near(k + 1, 1)
                second_part(k + 1, 1)

        if KEEP[2] == 32:
            got_near(k, 2)
        got_all(k, 2)

        @pl.when(k < 3)
        def _():
            new = tall[...] + times_turned(
                ltt.at[k, 0],
                [
                    jnp.concatenate([ed[k, o].reshape(128, 128), ed[k, o + 1].reshape(128, 128)], axis=1)
                    for o in range(0, NQ, 2)
                ],
            )
            put_x(k + 1, 0, -new.T)
            forward(k + 1, 1, 0, 7)

        for o in range(NQ):
            do[k, 128 * o : 128 * o + 128, :] = ed[k, o].reshape(128, 128).T
        pltpu.make_async_copy(do.at[k], out_d.at[k], o_sem.at[k, 2]).start()

        @pl.when(k < 2)
        def _():
            pick = rb[k + 2, 2 * q + 1] == rb[k + 1, 2 * q + 1]
            for o in range(NQ):
                lower = rb[k + 2, 2 * o + 1] == rb[k + 1, 2 * o + 1]
                span = slice(128 * o, 128 * o + 128)
                upper_part = jnp.where(pick, xsel[span, :], do[k, span, :])
                lower_part = jnp.where(pick, bsel[o], turn[k, o].T)
                bsel[o] = jnp.where(lower, lower_part, upper_part)
            held[...] = times_split(lsp.at[k + 1, 1], bsel[...].reshape(1024, 128))

        return carry

    lax.fori_loop(0, 4, step, 0)

    def finish(k):
        for c in range(3):
            sent(do.at[k, pl.ds(0, 992), :], ag_send.at[3 * k + c])
        for c in range(2):
            pltpu.make_async_copy(
                xo.at[k, c], out_x.at[k, :, :, :, pl.ds(128 * c, 128)], o_sem.at[k, c]
            ).wait()
        sent(gr.at[k, pl.ds(0, 7)], g_sem.at[k, 0])
        sent(lc.at[k, pl.ds(0, 7)], lc_send.at[k])
        pltpu.make_async_copy(do.at[k], out_d.at[k], o_sem.at[k, 2]).wait()

    loop(0, 4, finish)
    sent(cls.at[pl.ds(0, 3)], cls_sem.at[0])
    sent(lrow0.at[pl.ds(0, 7)], row0_sem.at[0])
    sent(lrow.at[pl.ds(0, 7)], row_sem.at[0])
    sent(lx.at[pl.ds(0, 7)], lx_sem.at[0])
    sent(xr.at[pl.ds(0, 7)], xr_sem.at[0])


def hand_over(xs, ds, out_x, out_d, buf_x, buf_d, in_sem, out_sem):
    reads, writes = [], []
    for k in range(4):
        for i in range(2):
            part = pl.ds(4 * i, 4)
            reads.append(pltpu.make_async_copy(xs.at[k, part], buf_x.at[k, part], in_sem.at[k, i]))
            writes.append(pltpu.make_async_copy(buf_x.at[k, part], out_x.at[k, part], out_sem.at[k, i]))
        reads.append(pltpu.make_async_copy(ds.at[k], buf_d.at[k], in_sem.at[k, 2]))
        writes.append(pltpu.make_async_copy(buf_d.at[k], out_d.at[k], out_sem.at[k, 2]))
    for read in reads:
        read.start()
    for read, write in zip(reads, writes):
        read.wait()
        write.start()
    for write in writes:
        write.wait()


def on_device(root_cov, row_blocks, lhat_t, diag_inv):
    anywhere = pl.BlockSpec(memory_space=pl.ANY)
    dma = pltpu.SemaphoreType.DMA
    vmem = pltpu.VMEM
    panels, diagonal = pl.pallas_call(
        kernel,
        out_shape=(
            jax.ShapeDtypeStruct((4, NZ, NX, 32, 256), F32),
            jax.ShapeDtypeStruct((4, 1024, 128), F32),
        ),
        in_specs=[pl.BlockSpec(memory_space=pltpu.SMEM), anywhere, anywhere, anywhere],
        out_specs=(anywhere, anywhere),
        scratch_shapes=[
            vmem((128, 512), F32),
            vmem((4, 32, 256), F32),
            vmem((4, 128, 128), F32),
            vmem((4, 128, 128), F32),
            vmem((4, 2, 128, 128), F32),
            vmem((8, 32, 256), F32),
            vmem((8, 3, 32, 256), F32),
            vmem((8, 32, 256), F32),
            vmem((2, 256, 128), F32),
            vmem((8, 2, 32, 128), F32),
            vmem((8, 2, 32, 128), F32),
            vmem((8, 128, 128), F32),
            vmem((1024, 128), F32),
            vmem((4, 8, 32, 256), F32),
            vmem((3, 2, 64, 1024), BF16),
            vmem((3, 2, 1024, 64), BF16),
            vmem((4, 2, 8, 4, 32, 128), F32),
            vmem((4, 8, 4, 32, 128), F32),
            vmem((4, 1024, 128), F32),
            vmem((3, 8, 128, 128), F32),
            vmem((4, 8, 32, 128), F32),
            vmem((4, 8, 32, 128), F32),
            vmem((32, 128), F32),
            vmem((128, 32), F32),
            dma((3,)),
            dma((2,)),
            dma((2,)),
            dma((2,)),
            dma((2,)),
            dma((2,)),
            dma((2,)),
            dma((4,)),
            dma((4, 2, 4)),
            dma((4, 2)),
            dma((3, 2)),
            dma((12, 8)),
            dma((12,)),
            dma((12,)),
            dma((12,)),
            dma((12,)),
            dma((4, 3)),
        ],
        compiler_params=pltpu.CompilerParams(
            collective_id=0, has_side_effects=True, vmem_limit_bytes=60 << 20
        ),
        name="selinv",
    )(row_blocks, root_cov, lhat_t, diag_inv)
    panels, diagonal = pl.pallas_call(
        hand_over,
        out_shape=(
            jax.ShapeDtypeStruct((4, NZ, NX, 32, 256), F32),
            jax.ShapeDtypeStruct((4, 1024, 128), F32),
        ),
        in_specs=[anywhere, anywhere],
        out_specs=(anywhere, anywhere),
        scratch_shapes=[
            vmem((4, NZ, NX, 32, 256), F32),
            vmem((4, 1024, 128), F32),
            dma((4, 3)),
            dma((4, 3)),
        ],
        compiler_params=pltpu.CompilerParams(vmem_limit_bytes=60 << 20),
        name="hand_over",
    )(panels, diagonal)
    return panels.reshape(4, 1024, 256), diagonal


def solution(mesh):
    return jax.shard_map(
        on_device,
        mesh=mesh,
        in_specs=(P("prow", "pcol"), P(), P(None, "prow", "pcol"), P(None, None, "pcol")),
        out_specs=(P(None, None, "pcol"), P(None, None, "pcol")),
        check_vma=False,
    )
```

time: 143 us -> 135 us (0.944); the launches traced: 141 us -> 135 us
  local copies, waits for them, and re-layouts: 6.04 us -> 0 us
    unnamed x4 -> x0, local copies, waits for them, and re-layouts: 6.04 us -> none
    pallas_call x1 -> x2, Pallas kernels: 134 us -> 134 us  [the longest x1 129 us: on_device(): pl.pallas_call(kernel, out_shape=(jax.ShapeDtypeStruct((4, NZ, NX, 32, 25...]
where the time goes in v3:
time: 135 us
  Pallas kernels  134 us (99%)
    pallas_call x1, Pallas kernels, on_device(): pl.pallas_call(kernel, out_shape=(jax.ShapeDtypeStruct((4, NZ, NX, 32, 25...  129 us
    pallas_call x1, Pallas kernels, on_device(): pl.pallas_call(hand_over, out_shape=(jax.ShapeDtypeStruct((4, NZ, NX, 32,...  5.46 us

profile of v3, /device:TPU:1, one launch (start us, length us, event | category | flops | bytes accessed | tf_op | source)
XLA Modules:
  0.0 134.8 jit_solution(11890179515719603883)
XLA Ops:
  0.6 128.7 %selinv.1 = (f32[4,8,4,32,256]{4,3,2,1,0:T(8,128)}, f32[4,1024,128]{2,1,0:T(8,128)}) custom-call(s32[4,16]{1,0:T(4,128)} %rb.1, f32[128,512]{1,0:T(8,128)} %root_h.1, f32[4,32,256]{2,1,0:T(8,128)} %lhat_h.1, f32[4,1024,128]{2,1,0:T(8,128)} %dinv_h.1), custom_call_target="tpu_custom_call" | custom-call | tf_op jit(solution)/shard_map/selinv/pallas_call | solution.py:462
  129.3 5.5 %hand_over.1 = (f32[4,8,4,32,256]{4,3,2,1,0:T(8,128)}, f32[4,1024,128]{2,1,0:T(8,128)}) custom-call(f32[4,8,4,32,256]{4,3,2,1,0:T(8,128)} %get-tuple-element.6.xs, f32[4,1024,128]{2,1,0:T(8,128)} %get-tuple-element.7.ds), custom_call_target="tpu_custom_call" | custom-call | tf_op jit(solution)/shard_map/hand_over/pallas_call | solution.py:518

commit v4 on v3

--- a/solution.py
+++ b/solution.py
@@ -113,13 +113,10 @@
     loads[1].wait()
     pl.semaphore_wait(barrier, NZ + NX + NQ)
 
-    def class_peer(e):
-        ref = cls.at[quarter]
-        copy_to(ref, ref, cls_sem.at[0], cls_sem.at[1], to_z(2 * e)).start()
-
-    class_peer(2)
-    class_peer(1)
-    class_peer(3)
+    for c in (1, 0):
+        ref = cls.at[quarter, c]
+        for e in (2, 1, 3):
+            copy_to(ref, ref, cls_sem.at[c, 0], cls_sem.at[c, 1], to_z(2 * e)).start()
     loop(1, NQ, lambda e: copy_to(lhat.at[0], lrow0.at[q], row0_sem.at[0], row0_sem.at[1], to_q(e)).start())
     loop(
         1, NQ,
@@ -185,7 +182,8 @@
     def start_gather(k, c):
         buf, n, keep = buf_of(k, c)
         ref = buf.at[z, x]
-        loop(1, NX, lambda e: copy_to(ref, ref, ag_send.at[n], c_recv.at[n], to_x(e)).start())
+        for e in (2, 1, 3):
+            copy_to(ref, ref, ag_send.at[n], c_recv.at[n], to_x(e)).start()
         top = buf.at[z, x, pl.ds(0, keep), :]
 
         def one(i):
@@ -230,9 +228,10 @@
 
     got(lx.at[pl.ds(0, 7)], lx_sem.at[1])
     left, left_low = halves(lx[...].reshape(256, 256))
-    got(cls.at[pl.ds(0, 3)], cls_sem.at[1])
-    lc_hop(0, 1)
-    for c in range(2):
+    for c in (1, 0):
+        got(cls.at[pl.ds(0, 3), c], cls_sem.at[c, 1])
+        if c == 0:
+            lc_hop(0, 1)
         for t in range(2):
             want = rb[0, 2 * g + t]
             blk = cls[0, c]
@@ -241,13 +240,12 @@
             az[c, 128 * t : 128 * t + 128, :] = blk
         hi, lo = halves(az[c])
         total = dot_nn(left, hi) + dot_nn(left_low, hi) + dot_nn(left, lo)
-        xp[:, c] = total.reshape(NQ, 32, 128)
-
-    def xp_peer(e):
-        to_group(e, lambda o, d: copy_to(xp.at[o], xr.at[g], xr_sem.at[0], xr_sem.at[1], d).start())
-
-    loop(1, NQ, xp_peer)
-    xr[g] = xp[g]
+        xp[c] = total.reshape(NQ, 32, 128)
+        for e in range(1, NQ):
+            to_group(
+                e, lambda o, d: copy_to(xp.at[c, o], xr.at[c, g], xr_sem.at[c, 0], xr_sem.at[c, 1], d).start()
+            )
+        xr[c, g] = xp[c, g]
 
     second = rb[1, 2 * q + 1] == rb[0, 2 * q + 1]
     low = rb[1, 2 * g + 1] == rb[0, 2 * g + 1]
@@ -259,19 +257,22 @@
     def b_peer(e):
         to_group(e, lambda o, d: copy_to(b_own, b_own, b_sem.at[0], b_sem.at[1], d).start())
 
+    def put_first(c):
+        got(xr.at[c, pl.ds(0, 7)], xr_sem.at[c, 1])
+        first = -xr[c, 0]
+        for o in range(1, NQ):
+            first = first - xr[c, o]
+        put_x(0, c, first)
+
+    put_first(1)
     loads[2].wait()
     loop(0, 4, turn_dinv)
     got(lrow.at[pl.ds(0, 7)], row_sem.at[1])
     prepare(0)
     prepare_t(0)
     lc_hop(0, 2)
-    got(xr.at[pl.ds(0, 7)], xr_sem.at[1])
-    first = -xr[0]
-    for o in range(1, NQ):
-        first = first - xr[o]
     lc_hop(0, 3)
-    put_x(0, 0, first[0])
-    put_x(0, 1, first[1])
+    put_first(0)
     loop(1, NQ, b_peer)
 
     def times_split(left_rows, value):
@@ -284,6 +285,8 @@
         for i, v in enumerate(lefts):
             acc = acc + dot_nn(stacked(v), right[256 * i : 256 * i + 256, :])
         return acc[0:128, 0:32] + acc[0:128, 32:64] + acc[128:256, 0:32]
+
+    forward(0, 1, 0, 7)
 
     def step(k, carry):
         if KEEP[1] == 32:
@@ -306,14 +309,14 @@
         def g_peer(e):
             copy_to(gs.at[k, (q + e) % NQ], gr.at[k, q], g_sem.at[k, 0], g_sem.at[k, 1], to_q(e)).start()
 
-        loop(1, NQ, g_peer)
+        for e in (4, 3, 5, 2, 6, 1, 7):
+            g_peer(e)
         gr[k, q] = gs[k, q]
         second_part(k, 0)
 
         @pl.when(k == 0)
         def _():
             second_part(k, 1)
-            forward(k, 1, 0, 7)
 
         forward(k, 0, 0, 7)
 
@@ -430,22 +433,29 @@
         pltpu.make_async_copy(do.at[k], out_d.at[k], o_sem.at[k, 2]).wait()
 
     loop(0, 4, finish)
-    sent(cls.at[pl.ds(0, 3)], cls_sem.at[0])
+    for c in range(2):
+        sent(cls.at[pl.ds(0, 3), c], cls_sem.at[c, 0])
+        sent(xr.at[c, pl.ds(0, 7)], xr_sem.at[c, 0])
     sent(lrow0.at[pl.ds(0, 7)], row0_sem.at[0])
     sent(lrow.at[pl.ds(0, 7)], row_sem.at[0])
     sent(lx.at[pl.ds(0, 7)], lx_sem.at[0])
-    sent(xr.at[pl.ds(0, 7)], xr_sem.at[0])
 
 
 def hand_over(xs, ds, out_x, out_d, buf_x, buf_d, in_sem, out_sem):
     reads, writes = [], []
+
+    def move(src, buf, dst):
+        n = len(reads)
+        reads.append(pltpu.make_async_copy(src, buf, in_sem.at[n]))
+        writes.append(pltpu.make_async_copy(buf, dst, out_sem.at[n]))
+
     for k in range(4):
-        for i in range(2):
-            part = pl.ds(4 * i, 4)
-            reads.append(pltpu.make_async_copy(xs.at[k, part], buf_x.at[k, part], in_sem.at[k, i]))
-            writes.append(pltpu.make_async_copy(buf_x.at[k, part], out_x.at[k, part], out_sem.at[k, i]))
-        reads.append(pltpu.make_async_copy(ds.at[k], buf_d.at[k], in_sem.at[k, 2]))
-        writes.append(pltpu.make_async_copy(buf_d.at[k], out_d.at[k], out_sem.at[k, 2]))
+        for o in range(0, NZ, 2):
+            part = pl.ds(o, 2)
+            move(xs.at[k, part], buf_x.at[k, part], out_x.at[k, part])
+        for o in range(0, 1024, 512):
+            part = pl.ds(o, 512)
+            move(ds.at[k, part], buf_d.at[k, part], out_d.at[k, part])
     for read in reads:
         read.start()
     for read, write in zip(reads, writes):
@@ -477,8 +487,8 @@
             vmem((8, 3, 32, 256), F32),
             vmem((8, 32, 256), F32),
             vmem((2, 256, 128), F32),
-            vmem((8, 2, 32, 128), F32),
-            vmem((8, 2, 32, 128), F32),
+            vmem((2, 8, 32, 128), F32),
+            vmem((2, 8, 32, 128), F32),
             vmem((8, 128, 128), F32),
             vmem((1024, 128), F32),
             vmem((4, 8, 32, 256), F32),
@@ -493,11 +503,11 @@
             vmem((32, 128), F32),
             vmem((128, 32), F32),
             dma((3,)),
+            dma((2, 2)),
             dma((2,)),
             dma((2,)),
             dma((2,)),
-            dma((2,)),
-            dma((2,)),
+            dma((2, 2)),
             dma((2,)),
             dma((4,)),
             dma((4, 2, 4)),
@@ -526,8 +536,8 @@
         scratch_shapes=[
             vmem((4, NZ, NX, 32, 256), F32),
             vmem((4, 1024, 128), F32),
-            dma((4, 3)),
-            dma((4, 3)),
+            dma((24,)),
+            dma((24,)),
         ],
         compiler_params=pltpu.CompilerParams(vmem_limit_bytes=60 << 20),
         name="hand_over",

time: 135 us -> 135 us (level)
  no operation moved by 1% of the time
where the time goes in v4:
time: 135 us
  Pallas kernels  134 us (99%)
    pallas_call x1, Pallas kernels, on_device(): pl.pallas_call(kernel, out_shape=(jax.ShapeDtypeStruct((4, NZ, NX, 32, 25...  128 us
    pallas_call x1, Pallas kernels, on_device(): pl.pallas_call(hand_over, out_shape=(jax.ShapeDtypeStruct((4, NZ, NX, 32,...  5.57 us

profile of v4, /device:TPU:1, one launch (start us, length us, event | category | flops | bytes accessed | tf_op | source)
XLA Modules:
  0.0 134.5 jit_solution(8841928998528787187)
XLA Ops:
  0.6 128.3 %selinv.1 = (f32[4,8,4,32,256]{4,3,2,1,0:T(8,128)}, f32[4,1024,128]{2,1,0:T(8,128)}) custom-call(s32[4,16]{1,0:T(4,128)} %rb.1, f32[128,512]{1,0:T(8,128)} %root_h.1, f32[4,32,256]{2,1,0:T(8,128)} %lhat_h.1, f32[4,1024,128]{2,1,0:T(8,128)} %dinv_h.1), custom_call_target="tpu_custom_call" | custom-call | tf_op jit(solution)/shard_map/selinv/pallas_call | solution.py:472
  129.0 5.6 %hand_over.1 = (f32[4,8,4,32,256]{4,3,2,1,0:T(8,128)}, f32[4,1024,128]{2,1,0:T(8,128)}) custom-call(f32[4,8,4,32,256]{4,3,2,1,0:T(8,128)} %get-tuple-element.6.xs, f32[4,1024,128]{2,1,0:T(8,128)} %get-tuple-element.7.ds), custom_call_target="tpu_custom_call" | custom-call | tf_op jit(solution)/shard_map/hand_over/pallas_call | solution.py:528

commit v5 on v4

--- a/solution.py
+++ b/solution.py
@@ -113,10 +113,12 @@
     loads[1].wait()
     pl.semaphore_wait(barrier, NZ + NX + NQ)
 
-    for c in (1, 0):
+    def send_class(c):
         ref = cls.at[quarter, c]
         for e in (2, 1, 3):
             copy_to(ref, ref, cls_sem.at[c, 0], cls_sem.at[c, 1], to_z(2 * e)).start()
+
+    send_class(1)
     loop(1, NQ, lambda e: copy_to(lhat.at[0], lrow0.at[q], row0_sem.at[0], row0_sem.at[1], to_q(e)).start())
     loop(
         1, NQ,
@@ -156,6 +158,7 @@
         )
 
     loop(1, NQ, lx_peer)
+    send_class(0)
     lx[g] = lrow0[g]
     lc_hop(0, 0)
 

time: 135 us -> 134 us (level)
  no operation moved by 1% of the time
where the time goes in v5:
time: 134 us
  Pallas kernels  133 us (99%)
    pallas_call x1, Pallas kernels, on_device(): pl.pallas_call(kernel, out_shape=(jax.ShapeDtypeStruct((4, NZ, NX, 32, 25...  128 us
    pallas_call x1, Pallas kernels, on_device(): pl.pallas_call(hand_over, out_shape=(jax.ShapeDtypeStruct((4, NZ, NX, 32,...  5.57 us

profile of v5, /device:TPU:1, one launch (start us, length us, event | category | flops | bytes accessed | tf_op | source)
XLA Modules:
  0.0 134.0 jit_solution(16427745784118554938)
XLA Ops:
  0.6 127.8 %selinv.1 = (f32[4,8,4,32,256]{4,3,2,1,0:T(8,128)}, f32[4,1024,128]{2,1,0:T(8,128)}) custom-call(s32[4,16]{1,0:T(4,128)} %rb.1, f32[128,512]{1,0:T(8,128)} %root_h.1, f32[4,32,256]{2,1,0:T(8,128)} %lhat_h.1, f32[4,1024,128]{2,1,0:T(8,128)} %dinv_h.1), custom_call_target="tpu_custom_call" | custom-call | tf_op jit(solution)/shard_map/selinv/pallas_call | solution.py:475
  128.5 5.6 %hand_over.1 = (f32[4,8,4,32,256]{4,3,2,1,0:T(8,128)}, f32[4,1024,128]{2,1,0:T(8,128)}) custom-call(f32[4,8,4,32,256]{4,3,2,1,0:T(8,128)} %get-tuple-element.6.xs, f32[4,1024,128]{2,1,0:T(8,128)} %get-tuple-element.7.ds), custom_call_target="tpu_custom_call" | custom-call | tf_op jit(solution)/shard_map/hand_over/pallas_call | solution.py:531
